TPU v7x, 128 devices: a whole 4x4x4 slice. The times are simulated.
128 devices in a mesh: src: 8 (over x, z_hi), tgt: 16 (over y, z_lo, core).
Axes of the slice: x: 4, y: 4, z: 4 (z_hi: 2, z_lo: 2; z = z_hi * 2 + z_lo), core: 2. Of those that a mesh axis runs over, the one named last changes fastest.
Arguments:
- noise: bfloat16 [4096, 2048], P(('src', 'tgt')), may hold values from -6 to 6
- data: bfloat16 [4096, 2048], P(('src', 'tgt')), may hold values from -6 to 6
- t_index: int32 [4096], P(('src', 'tgt')), may hold values from 0 to 1000
- embed_weight: bfloat16 [64, 2048], replicated, may hold values from -0.75 to 0.75
- position: bfloat16 [32, 2048], replicated, may hold values from -6 to 6
- norm_gain: float32 [2048], replicated, may hold values from 0.5 to 1.5
- qkv_weight: bfloat16 [2048, 6144], P(None, 'tgt'), may hold values from -0.125 to 0.125
Outputs:
- velocity: bfloat16 [4096, 2048], P(('src', 'tgt'))
- qkv: bfloat16 [131072, 6144], P(('src', 'tgt'))
All inputs are finite; a program needn't handle non-finite values.
Results may differ from a plain program's by a relative error of at most 0.014.
Values may be sent and summed in bfloat16 or wider, within the bound.
No kernel may reach another device: no remote copies, remote signals or barrier semaphores. Data moves between devices by JAX's collectives and lax.ppermute only.
A program may use at most 448 MiB of HBM per device.

v0:
```python
import jax
import jax.numpy as jnp
from jax import lax
from jax.sharding import PartitionSpec as P

ITERS = 3
TGRID = 1000


def shared(value, axis, count):
    spread = lax.optimization_barrier(jnp.broadcast_to(value[None], (count,) + value.shape))
    return lax.all_to_all(spread, axis, 0, 0)


def lse(scores, dim):
    peak = jnp.max(scores, axis=dim, keepdims=True)
    total = jnp.sum(jnp.exp(scores - peak), axis=dim)
    return jnp.squeeze(peak, dim) + jnp.log(total)


def halves(value):
    high = value.astype(jnp.bfloat16)
    low = (value - high.astype(jnp.float32)).astype(jnp.bfloat16)
    return (high, low)


def folded_weights(embed_weight, position, norm_gain, qkv_weight):
    scaled = jnp.concatenate([embed_weight, position], 0).astype(jnp.float32) * norm_gain
    high, low = halves(scaled)
    both = jnp.dot(jnp.concatenate([high, low], 0), qkv_weight, preferred_element_type=jnp.float32)
    rows = scaled.shape[0]
    return jnp.concatenate(halves(both[:rows] + both[rows:]), 0)


def local(noise, data, t_index, embed_weight, position, norm_gain, qkv_weight):
    latent = noise.shape[1]
    own = noise.shape[0]
    n_src = lax.axis_size("src")
    n_tgt = lax.axis_size("tgt")
    folded = lax.all_gather(
        folded_weights(embed_weight, position, norm_gain, qkv_weight), "tgt", axis=1, tiled=True
    )
    noise_block = lax.all_gather(noise, "tgt", axis=0, tiled=True)
    data_block = lax.all_gather(data, "src", axis=0, tiled=True)
    noise_sq = jnp.sum(jnp.square(noise_block.astype(jnp.float32)), axis=1)
    data_sq = jnp.sum(jnp.square(data_block.astype(jnp.float32)), axis=1)
    cross_term = lax.dot_general(
        noise_block, data_block, (((1,), (1,)), ((), ())), preferred_element_type=jnp.float32
    )
    cost = (noise_sq[:, None] + data_sq[None, :] - 2.0 * cross_term) / latent
    col_pot = jnp.zeros((data_block.shape[0],), jnp.float32)
    epsilon = 0.04
    for step in range(ITERS):
        epsilon = 0.04 * 0.45**step
        part = lse((col_pot[None, :] - cost) / epsilon, 1)
        row_pot = -epsilon * lse(shared(part, "tgt", n_tgt), 0)
        part = lse((row_pot[:, None] - cost) / epsilon, 0)
        col_pot = -epsilon * lse(shared(part, "src", n_src), 0)
    scores = (col_pot[None, :] - cost) / epsilon
    total = lse(shared(lse(scores, 1), "tgt", n_tgt), 0)
    coupling = jnp.exp(scores - total[:, None]).astype(jnp.bfloat16)
    partial_sum = jnp.dot(coupling, data_block, preferred_element_type=jnp.float32)
    pieces = lax.all_to_all(
        partial_sum.astype(jnp.bfloat16).reshape(n_tgt, own, latent), "tgt", 0, 0
    )
    target = jnp.sum(pieces.astype(jnp.float32), axis=0)
    noise_own = noise.astype(jnp.float32)
    velocity = (target - noise_own).astype(jnp.bfloat16)
    times = t_index.astype(jnp.float32) / TGRID
    mixed = ((1.0 - times)[:, None] * noise_own + times[:, None] * target).astype(jnp.bfloat16)
    patch_in, width = embed_weight.shape
    patch_count = position.shape[0]
    patches = mixed.reshape(own * patch_count, patch_in)
    embedded = jnp.dot(patches, embed_weight, preferred_element_type=jnp.float32)
    embedded = embedded.reshape(own, patch_count, width) + position.astype(jnp.float32)[None]
    scale = lax.rsqrt(jnp.mean(embedded * embedded, axis=-1) + 1e-06).reshape(own * patch_count)
    place = jnp.tile(jnp.eye(patch_count, dtype=jnp.bfloat16), (own, 1))
    tokens = jnp.concatenate([patches, place, patches, place], 1)
    qkv = jnp.dot(tokens, folded, preferred_element_type=jnp.float32) * scale[:, None]
    return (velocity, qkv.astype(jnp.bfloat16))


def solution(mesh):
    return jax.shard_map(
        local,
        mesh=mesh,
        in_specs=(
            P(("src", "tgt"), None),
            P(("src", "tgt"), None),
            P(("src", "tgt")),
            P(),
            P(),
            P(),
            P(None, "tgt"),
        ),
        out_specs=(P(("src", "tgt"), None), P(("src", "tgt"), None)),
        check_vma=False,
    )
```

profile of v0, /device:TPU:33, one launch (start us, length us, event | category | flops | bytes accessed | tf_op | source)
XLA Modules:
  0.0 236.3 jit_solution(10667740617140354199)
XLA Ops:
  7.2 0.7 all-gather.6.cloned.1.call-update
  8.0 0.7 all-gather.4.cloned.1.call-update
  8.7 49.3 %all-gather.6.cloned.1.call-done = bf16[256,2048]{1,0:T(8,128)(2,1)} async-done(((bf16[32,2048]{1,0:T(8,128)(2,1)}), bf16[256,2048]{1,0:T(8,128)(2,1)}) %all-gather.6.cloned.1.call-update) | async-done | bytes 1048592 | tf_op jit(solution)/shard_map/all_gather | solution.py:44
  58.0 1.6 multiply_reduce_fusion.2
  59.6 34.7 %all-gather.4.cloned.1.call-done = bf16[512,2048]{1,0:T(8,128)(2,1)} async-done(((bf16[32,2048]{1,0:T(8,128)(2,1)}), bf16[512,2048]{1,0:T(8,128)(2,1)}) %all-gather.4.cloned.1.call-update) | async-done | bytes 2097168 | tf_op jit(solution)/shard_map/all_gather | solution.py:43
  94.3 2.2 multiply_reduce_fusion.1
  96.6 0.9 fusion.14
  97.7 9.3 %all_to_all.89 = f32[16,1,512]{2,1,0:T(1,128)S(1)} all-to-all(f32[16,1,512]{2,1,0:T(1,128)S(1)} %all_to_all.59), channel_id=1, replica_groups=mesh['src'=8,'tgt'=16] {'tgt'}, dimensions={0} | all-to-all | bytes 65536 | tf_op jit(solution)/shard_map/all_to_all | solution.py:12
  107.5 11.8 %all_to_all.90 = f32[8,1,256]{2,1,0:T(1,128)S(1)} all-to-all(f32[8,1,256]{2,1,0:T(1,128)S(1)} %all_to_all.62), channel_id=1, replica_groups=mesh['src'=8,'tgt'=16] {'src'}, dimensions={0} | all-to-all | bytes 16384 | tf_op jit(solution)/shard_map/all_to_all | solution.py:12
  119.7 0.6 all_to_all.65
  120.4 6.8 %all-to-all-start.2 = ((f32[16,1,512]{2,1,0:T(1,128)}), f32[16,1,512]{2,1,0:T(1,128)S(1)}, u32[]{:S(2)}, u32[]{:S(2)}) async-start(f32[16,1,512]{2,1,0:T(1,128)} %all_to_all.65), calls=%async_computation.2 | async-start | bytes 65536 | tf_op jit(solution)/shard_map/all_to_all | solution.py:12
  127.2 2.0 fusion.6
  129.1 2.8 %all-to-all-done.2 = f32[16,1,512]{2,1,0:T(1,128)S(1)} async-done(((f32[16,1,512]{2,1,0:T(1,128)}), f32[16,1,512]{2,1,0:T(1,128)S(1)}, u32[]{:S(2)}, u32[]{:S(2)}) %all-to-all-start.2) | async-done | bytes 32800 | tf_op jit(solution)/shard_map/all_to_all | solution.py:12
  133.0 3.3 %all-to-all-start.3 = ((f32[8,1,256]{2,1,0:T(1,128)}), f32[8,1,256]{2,1,0:T(1,128)S(1)}, u32[]{:S(2)}, u32[]{:S(2)}) async-start(f32[8,1,256]{2,1,0:T(1,128)} %all_to_all.68), calls=%async_computation.3 | async-start | bytes 16384 | tf_op jit(solution)/shard_map/all_to_all | solution.py:12
  136.4 2.4 %fusion.2 = f32[192,384]{1,0:T(8,128)} fusion(bf16[2048,384]{1,0:T(8,128)(2,1)S(1)} %copy-done, bf16[96,2048]{1,0:T(8,128)(2,1)} %get-tuple-element.5, bf16[96,2048]{1,0:T(8,128)(2,1)} %get-tuple-element.4), kind=kOutput, calls=%fused_computation.9 | convolution fusion | flops 303562752 | bytes 2654208 | tf_op jit(solution)/shard_map/dot_general | solution.py:30
  138.8 4.0 %all-to-all-done.3 = f32[8,1,256]{2,1,0:T(1,128)S(1)} async-done(((f32[8,1,256]{2,1,0:T(1,128)}), f32[8,1,256]{2,1,0:T(1,128)S(1)}, u32[]{:S(2)}, u32[]{:S(2)}) %all-to-all-start.3) | async-done | bytes 8224 | tf_op jit(solution)/shard_map/all_to_all | solution.py:12
  143.2 0.6 all_to_all.71
  143.9 5.9 %all-to-all-start.4 = ((f32[16,1,512]{2,1,0:T(1,128)}), f32[16,1,512]{2,1,0:T(1,128)S(1)}, u32[]{:S(2)}, u32[]{:S(2)}) async-start(f32[16,1,512]{2,1,0:T(1,128)} %all_to_all.71), calls=%async_computation.4 | async-start | bytes 65536 | tf_op jit(solution)/shard_map/all_to_all | solution.py:12
  149.8 1.0 subtract_convert_fusion.1
  150.8 3.8 %all-to-all-done.4 = f32[16,1,512]{2,1,0:T(1,128)S(1)} async-done(((f32[16,1,512]{2,1,0:T(1,128)}), f32[16,1,512]{2,1,0:T(1,128)S(1)}, u32[]{:S(2)}, u32[]{:S(2)}) %all-to-all-start.4) | async-done | bytes 32800 | tf_op jit(solution)/shard_map/all_to_all | solution.py:12
  155.1 0.6 all_to_all.74
  155.7 3.3 %all-to-all-start.5 = ((f32[8,1,256]{2,1,0:T(1,128)}), f32[8,1,256]{2,1,0:T(1,128)S(1)}, u32[]{:S(2)}, u32[]{:S(2)}) async-start(f32[8,1,256]{2,1,0:T(1,128)} %all_to_all.74), calls=%async_computation.5 | async-start | bytes 16384 | tf_op jit(solution)/shard_map/all_to_all | solution.py:12
  159.1 0.7 pad_maximum_fusion.1
  159.8 5.7 %all-to-all-done.5 = f32[8,1,256]{2,1,0:T(1,128)S(1)} async-done(((f32[8,1,256]{2,1,0:T(1,128)}), f32[8,1,256]{2,1,0:T(1,128)S(1)}, u32[]{:S(2)}, u32[]{:S(2)}) %all-to-all-start.5) | async-done | bytes 8224 | tf_op jit(solution)/shard_map/all_to_all | solution.py:12
  165.9 9.8 %all_to_all.91 = f32[16,1,512]{2,1,0:T(1,128)S(1)} all-to-all(f32[16,1,512]{2,1,0:T(1,128)S(1)} %all_to_all.77), channel_id=1, replica_groups=mesh['src'=8,'tgt'=16] {'tgt'}, dimensions={0} | all-to-all | bytes 65536 | tf_op jit(solution)/shard_map/all_to_all | solution.py:12
  175.8 2.2 convolution_convert_fusion
  178.0 5.8 %all-to-all-start.7 = ((bf16[16,32,2048]{2,1,0:T(8,128)(2,1)}), bf16[16,32,2048]{2,1,0:T(8,128)(2,1)}, u32[]{:S(2)}, u32[]{:S(2)}) async-start(bf16[16,32,2048]{2,1,0:T(8,128)(2,1)} %bitcast.53), calls=%async_computation.7 | async-start | bytes 4194304 | tf_op jit(solution)/shard_map/all_to_all | solution.py:63
  183.9 32.7 %all-to-all-done.7 = bf16[16,32,2048]{2,1,0:T(8,128)(2,1)} async-done(((bf16[16,32,2048]{2,1,0:T(8,128)(2,1)}), bf16[16,32,2048]{2,1,0:T(8,128)(2,1)}, u32[]{:S(2)}, u32[]{:S(2)}) %all-to-all-start.7) | async-done | bytes 2097184 | tf_op jit(solution)/shard_map/all_to_all | solution.py:63
  216.6 2.0 convert_reduce_fusion
  218.6 0.7 fusion.23
  219.8 1.3 multiply_reduce_fusion
  221.3 8.5 %multiply_convert_fusion = bf16[1024,6144]{1,0:T(8,128)(2,1)} fusion(f32[1024]{0:T(1024)S(1)} %rsqrt.11, bf16[192,6144]{1,0:T(8,128)(2,1)} %all-gather.8.cloned.1.call-done, bf16[1024,32]{1,0:T(8,128)(2,1)S(1)} %bitcast.54, bf16[1024,64]{1,0:T(8,128)(2,1)S(1)} %reshape.161), kind=kOutput, calls=%fused_computation | convolution fusion | flops 2430074880 | bytes 15142912 | tf_op jit(solution)/shard_map/dot_general | solution.py:79
  (81 shorter events, 4.3 us)
Async XLA Ops:
  7.2 129.2 %copy-start = (bf16[2048,384]{1,0:T(8,128)(2,1)S(1)}, bf16[2048,384]{1,0:T(8,128)(2,1)}, u32[]{:S(2)}) copy-start(bf16[2048,384]{1,0:T(8,128)(2,1)} %param.13) | copy-start | bytes 4718596
  7.2 50.8 %all-gather.6.cloned.1.call-start = ((), (), s32[]{:S(2)}) async-start(), calls=%async_computation.9 | async-start | bytes 1179648 | tf_op jit(solution)/shard_map/all_gather | solution.py:44
  7.9 86.4 %all-gather.4.cloned.1.call-start = ((), (), s32[]{:S(2)}) async-start(), calls=%async_computation.8 | async-start | bytes 2228224 | tf_op jit(solution)/shard_map/all_gather | solution.py:43
  58.0 38.6 %copy-start.1 = (bf16[256,2048]{1,0:T(8,128)(2,1)S(1)}, bf16[256,2048]{1,0:T(8,128)(2,1)}, u32[]{:S(2)}) copy-start(bf16[256,2048]{1,0:T(8,128)(2,1)} %all-gather.6.cloned.1.call-done) | copy-start | bytes 3145732
  94.3 2.2 copy-start.2
  97.5 29.6 %copy-start.3 = (bf16[32,2048]{1,0:T(8,128)(2,1)S(1)}, bf16[32,2048]{1,0:T(8,128)(2,1)}, u32[]{:S(2)}) copy-start(bf16[32,2048]{1,0:T(8,128)(2,1)} %param.11) | copy-start | bytes 393220
  97.5 29.6 %copy-start.6 = (f32[2048]{0:T(1024)S(1)}, f32[2048]{0:T(1024)}, u32[]{:S(2)}) copy-start(f32[2048]{0:T(1024)} %param.12) | copy-start | bytes 24580
  120.4 11.6 %all-to-all-start.2 = ((f32[16,1,512]{2,1,0:T(1,128)}), f32[16,1,512]{2,1,0:T(1,128)S(1)}, u32[]{:S(2)}, u32[]{:S(2)}) async-start(f32[16,1,512]{2,1,0:T(1,128)} %all_to_all.65), calls=%async_computation.2 | async-start | bytes 65536 | tf_op jit(solution)/shard_map/all_to_all | solution.py:12
  133.0 9.8 %all-to-all-start.3 = ((f32[8,1,256]{2,1,0:T(1,128)}), f32[8,1,256]{2,1,0:T(1,128)S(1)}, u32[]{:S(2)}, u32[]{:S(2)}) async-start(f32[8,1,256]{2,1,0:T(1,128)} %all_to_all.68), calls=%async_computation.3 | async-start | bytes 16384 | tf_op jit(solution)/shard_map/all_to_all | solution.py:12
  143.9 10.7 %all-to-all-start.4 = ((f32[16,1,512]{2,1,0:T(1,128)}), f32[16,1,512]{2,1,0:T(1,128)S(1)}, u32[]{:S(2)}, u32[]{:S(2)}) async-start(f32[16,1,512]{2,1,0:T(1,128)} %all_to_all.71), calls=%async_computation.4 | async-start | bytes 65536 | tf_op jit(solution)/shard_map/all_to_all | solution.py:12
  155.7 9.8 %all-to-all-start.5 = ((f32[8,1,256]{2,1,0:T(1,128)}), f32[8,1,256]{2,1,0:T(1,128)S(1)}, u32[]{:S(2)}, u32[]{:S(2)}) async-start(f32[8,1,256]{2,1,0:T(1,128)} %all_to_all.74), calls=%async_computation.5 | async-start | bytes 16384 | tf_op jit(solution)/shard_map/all_to_all | solution.py:12
  159.0 62.2 %all-gather.8.cloned.1.call-start = ((), (), s32[]{:S(2)}) async-start(), calls=%async_computation.10 | async-start | bytes 2506752 | tf_op jit(solution)/shard_map/all_gather | solution.py:40
  178.0 5.8 %copy-start.7 = (s32[32]{0:T(128)S(1)}, s32[32]{0:T(128)}, u32[]{:S(2)}) copy-start(s32[32]{0:T(128)} %param.9) | copy-start | bytes 388
  178.0 38.6 %all-to-all-start.7 = ((bf16[16,32,2048]{2,1,0:T(8,128)(2,1)}), bf16[16,32,2048]{2,1,0:T(8,128)(2,1)}, u32[]{:S(2)}, u32[]{:S(2)}) async-start(bf16[16,32,2048]{2,1,0:T(8,128)(2,1)} %bitcast.53), calls=%async_computation.7 | async-start | bytes 4194304 | tf_op jit(solution)/shard_map/all_to_all | solution.py:63
  183.8 34.8 %copy-start.4 = (bf16[32,2048]{1,0:T(8,128)(2,1)S(1)}, bf16[32,2048]{1,0:T(8,128)(2,1)}, u32[]{:S(2)}) copy-start(bf16[32,2048]{1,0:T(8,128)(2,1)} %param.7) | copy-start | bytes 393220
  183.8 36.0 %copy-start.5 = (bf16[64,2048]{1,0:T(8,128)(2,1)S(1)}, bf16[64,2048]{1,0:T(8,128)(2,1)}, u32[]{:S(2)}) copy-start(bf16[64,2048]{1,0:T(8,128)(2,1)} %param.10) | copy-start | bytes 786436
Sparse Core Ops, SparseCore 0:
  10.4 47.5 all-gather.5
  59.7 34.5 all-gather.3
  161.5 46.7 all-gather.7
where the time goes:
time: 237 us; the launch traced here: 236 us
  waiting for transfers between devices  135 us (57%)
  blocking collectives  30.9 us (13%)
  starting transfers between devices  25.2 us (11%)
  matrix products  15.3 us (6%)
  between operations  14.1 us (6%)
  other arithmetic  13 us (5%)
  local copies, waits for them, and re-layouts  3.21 us (1%)
    all_gather x1, waiting for transfers between devices, local(): data_block = lax.all_gather(data, 'src', axis=0, tiled=True)  49.3 us
    all_gather x1, waiting for transfers between devices, local(): noise_block = lax.all_gather(noise, 'tgt', axis=0, tiled=True)  34.7 us
    all_to_all x1, waiting for transfers between devices, local(): lax.all_to_all(partial_sum.astype(jnp.bfloat16).reshape(n_tgt, own, laten...  32.7 us
    all_to_all x3, blocking collectives, shared(): return lax.all_to_all(spread, axis, 0, 0)  30.9 us
    all_to_all x4, starting transfers between devices, shared(): return lax.all_to_all(spread, axis, 0, 0)  19.4 us
    all_to_all x4, waiting for transfers between devices, shared(): return lax.all_to_all(spread, axis, 0, 0)  16.4 us
    dot_general x1, matrix products, local(): jnp.dot(tokens, folded, preferred_element_type=jnp.float32) * scale[:, None]  8.46 us
    all_to_all x1, starting transfers between devices, local(): lax.all_to_all(partial_sum.astype(jnp.bfloat16).reshape(n_tgt, own, laten...  5.76 us
  transfers between devices with their start and end apart: 8, of which 7 were waited for; matrix products, arithmetic and copies ran while one was open for 6% of the time, Pallas kernels for 0%

commit v1 on v0

--- a/solution.py
+++ b/solution.py
@@ -40,7 +40,9 @@
     folded = lax.all_gather(
         folded_weights(embed_weight, position, norm_gain, qkv_weight), "tgt", axis=1, tiled=True
     )
-    noise_block = lax.all_gather(noise, "tgt", axis=0, tiled=True)
+    noise_block = jnp.concatenate(
+        lax.all_to_all(jnp.stack([noise] * lax.axis_size("tgt")), "tgt", 0, 0), axis=0
+    )
     data_block = lax.all_gather(data, "src", axis=0, tiled=True)
     noise_sq = jnp.sum(jnp.square(noise_block.astype(jnp.float32)), axis=1)
     data_sq = jnp.sum(jnp.square(data_block.astype(jnp.float32)), axis=1)

time: 237 us -> 217 us (0.916)
  waiting for transfers between devices: 135 us -> 102 us
  starting transfers between devices: 25.2 us -> 31.5 us
  local copies, waits for them, and re-layouts: 3.21 us -> 5.77 us
    all_gather x1 -> x0, waiting for transfers between devices: 34.7 us -> none  [local(): noise_block = lax.all_gather(noise, 'tgt', axis=0, tiled=True)]
    all_to_all x0 -> x1, starting transfers between devices: none -> 6.26 us  [local(): lax.all_to_all(jnp.stack([noise] * lax.axis_size('tgt')), 'tgt', 0, 0)]
    another operation x0 -> x1, local copies, waits for them, and re-layouts: none -> 2.48 us  [local(): jnp.stack([noise] * lax.axis_size('tgt'))]
    all_gather x1, waiting for transfers between devices: 49.3 us -> 51.8 us  [local(): data_block = lax.all_gather(data, 'src', axis=0, tiled=True)]
  transfers between devices with their start and end apart: 8 -> 8, of which waited for: 7 -> 6; matrix products, arithmetic and copies ran while one was open for 6% -> 8% of each run, Pallas kernels for 0% -> 0%
where the time goes in v1:
time: 217 us; the launch traced here: 216 us
  waiting for transfers between devices  102 us (47%)
  blocking collectives  31.9 us (15%)
  starting transfers between devices  31.5 us (15%)
  matrix products  16.8 us (8%)
  between operations  15.8 us (7%)
  other arithmetic  12.8 us (6%)
  local copies, waits for them, and re-layouts  5.77 us (3%)
    all_gather x1, waiting for transfers between devices, local(): data_block = lax.all_gather(data, 'src', axis=0, tiled=True)  51.8 us
    all_to_all x1, waiting for transfers between devices, local(): lax.all_to_all(partial_sum.astype(jnp.bfloat16).reshape(n_tgt, own, laten...  33.2 us
    all_to_all x3, blocking collectives, shared(): return lax.all_to_all(spread, axis, 0, 0)  31.9 us
    all_to_all x4, starting transfers between devices, shared(): return lax.all_to_all(spread, axis, 0, 0)  19.4 us
    all_to_all x4, waiting for transfers between devices, shared(): return lax.all_to_all(spread, axis, 0, 0)  16.4 us
    dot_general x1, matrix products, local(): jnp.dot(tokens, folded, preferred_element_type=jnp.float32) * scale[:, None]  8.46 us
    all_to_all x1, starting transfers between devices, local(): lax.all_to_all(jnp.stack([noise] * lax.axis_size('tgt')), 'tgt', 0, 0)  6.26 us
    all_to_all x1, starting transfers between devices, local(): lax.all_to_all(partial_sum.astype(jnp.bfloat16).reshape(n_tgt, own, laten...  5.77 us
  transfers between devices with their start and end apart: 8, of which 6 were waited for; matrix products, arithmetic and copies ran while one was open for 8% of the time, Pallas kernels for 0%

profile of v1, /device:TPU:33, one launch (start us, length us, event | category | flops | bytes accessed | tf_op | source)
XLA Modules:
  0.0 216.5 jit_solution(6961906513983472249)
XLA Ops:
  8.1 0.7 all-gather.3.cloned.1.call-update
  8.7 2.5 %stack.2 = bf16[16,32,2048]{2,1,0:T(8,128)(2,1)} broadcast(bf16[32,2048]{1,0:T(8,128)(2,1)} %param.7), dimensions={1,2} | broadcast | bytes 2228224 | tf_op jit(solution)/shard_map/stack | solution.py:44
  11.2 6.3 %all-to-all-start = ((bf16[16,32,2048]{2,1,0:T(8,128)(2,1)}), bf16[16,32,2048]{2,1,0:T(8,128)(2,1)}, u32[]{:S(2)}, u32[]{:S(2)}) async-start(bf16[16,32,2048]{2,1,0:T(8,128)(2,1)} %stack.2), calls=%async_computation | async-start | bytes 4194304 | tf_op jit(solution)/shard_map/all_to_all | solution.py:44
  17.5 51.8 %all-gather.3.cloned.1.call-done = bf16[256,2048]{1,0:T(8,128)(2,1)} async-done(((bf16[32,2048]{1,0:T(8,128)(2,1)}), bf16[256,2048]{1,0:T(8,128)(2,1)}) %all-gather.3.cloned.1.call-update) | async-done | bytes 1048592 | tf_op jit(solution)/shard_map/all_gather | solution.py:46
  69.3 1.6 multiply_reduce_fusion.2
  70.9 2.1 multiply_reduce_fusion.1
  73.0 2.4 %fusion.14 = (f32[512]{0:T(512)S(1)}, f32[512,256]{0,1:T(8,128)S(1)}) fusion(bf16[512,2048]{1,0:T(8,128)(2,1)} %bitcast, bf16[256,2048]{1,0:T(8,128)(2,1)S(1)} %copy-done.1, f32[256]{0:T(256)S(1)} %multiply_reduce_fusion.2, f32[512]{0:T(512)S(1)} %add.138), kind=kOutput, calls=%fused_computation.38 | convolution fusion | flops 537787904 | bytes 3675136 | tf_op jit(solution)/shard_map/dot_general | solution.py:49
  75.6 11.5 %all_to_all.94 = f32[16,1,512]{2,1,0:T(1,128)S(1)} all-to-all(f32[16,1,512]{2,1,0:T(1,128)S(1)} %all_to_all.63), channel_id=1, replica_groups=mesh['src'=8,'tgt'=16] {'tgt'}, dimensions={0} | all-to-all | bytes 65536 | tf_op jit(solution)/shard_map/all_to_all | solution.py:12
  87.7 10.5 %all_to_all.95 = f32[8,1,256]{2,1,0:T(1,128)S(1)} all-to-all(f32[8,1,256]{2,1,0:T(1,128)S(1)} %all_to_all.66), channel_id=1, replica_groups=mesh['src'=8,'tgt'=16] {'src'}, dimensions={0} | all-to-all | bytes 16384 | tf_op jit(solution)/shard_map/all_to_all | solution.py:12
  98.6 0.6 all_to_all.69
  99.2 6.8 %all-to-all-start.3 = ((f32[16,1,512]{2,1,0:T(1,128)}), f32[16,1,512]{2,1,0:T(1,128)S(1)}, u32[]{:S(2)}, u32[]{:S(2)}) async-start(f32[16,1,512]{2,1,0:T(1,128)} %all_to_all.69), calls=%async_computation.3 | async-start | bytes 65536 | tf_op jit(solution)/shard_map/all_to_all | solution.py:12
  106.0 2.0 fusion.6
  108.0 2.8 %all-to-all-done.3 = f32[16,1,512]{2,1,0:T(1,128)S(1)} async-done(((f32[16,1,512]{2,1,0:T(1,128)}), f32[16,1,512]{2,1,0:T(1,128)S(1)}, u32[]{:S(2)}, u32[]{:S(2)}) %all-to-all-start.3) | async-done | bytes 32800 | tf_op jit(solution)/shard_map/all_to_all | solution.py:12
  111.9 3.3 %all-to-all-start.4 = ((f32[8,1,256]{2,1,0:T(1,128)}), f32[8,1,256]{2,1,0:T(1,128)S(1)}, u32[]{:S(2)}, u32[]{:S(2)}) async-start(f32[8,1,256]{2,1,0:T(1,128)} %all_to_all.72), calls=%async_computation.4 | async-start | bytes 16384 | tf_op jit(solution)/shard_map/all_to_all | solution.py:12
  115.2 2.4 %fusion.2 = f32[192,384]{1,0:T(8,128)} fusion(bf16[2048,384]{1,0:T(8,128)(2,1)S(1)} %copy-done, bf16[96,2048]{1,0:T(8,128)(2,1)} %get-tuple-element.5, bf16[96,2048]{1,0:T(8,128)(2,1)} %get-tuple-element.4), kind=kOutput, calls=%fused_computation.9 | convolution fusion | flops 303562752 | bytes 2654208 | tf_op jit(solution)/shard_map/dot_general | solution.py:30
  117.6 4.0 %all-to-all-done.4 = f32[8,1,256]{2,1,0:T(1,128)S(1)} async-done(((f32[8,1,256]{2,1,0:T(1,128)}), f32[8,1,256]{2,1,0:T(1,128)S(1)}, u32[]{:S(2)}, u32[]{:S(2)}) %all-to-all-start.4) | async-done | bytes 8224 | tf_op jit(solution)/shard_map/all_to_all | solution.py:12
  122.1 0.6 all_to_all.75
  122.7 5.9 %all-to-all-start.5 = ((f32[16,1,512]{2,1,0:T(1,128)}), f32[16,1,512]{2,1,0:T(1,128)S(1)}, u32[]{:S(2)}, u32[]{:S(2)}) async-start(f32[16,1,512]{2,1,0:T(1,128)} %all_to_all.75), calls=%async_computation.5 | async-start | bytes 65536 | tf_op jit(solution)/shard_map/all_to_all | solution.py:12
  128.7 1.0 subtract_convert_fusion.1
  129.7 3.8 %all-to-all-done.5 = f32[16,1,512]{2,1,0:T(1,128)S(1)} async-done(((f32[16,1,512]{2,1,0:T(1,128)}), f32[16,1,512]{2,1,0:T(1,128)S(1)}, u32[]{:S(2)}, u32[]{:S(2)}) %all-to-all-start.5) | async-done | bytes 32800 | tf_op jit(solution)/shard_map/all_to_all | solution.py:12
  133.9 0.6 all_to_all.78
  134.5 3.3 %all-to-all-start.6 = ((f32[8,1,256]{2,1,0:T(1,128)}), f32[8,1,256]{2,1,0:T(1,128)S(1)}, u32[]{:S(2)}, u32[]{:S(2)}) async-start(f32[8,1,256]{2,1,0:T(1,128)} %all_to_all.78), calls=%async_computation.6 | async-start | bytes 16384 | tf_op jit(solution)/shard_map/all_to_all | solution.py:12
  137.9 0.7 pad_maximum_fusion.1
  138.6 5.7 %all-to-all-done.6 = f32[8,1,256]{2,1,0:T(1,128)S(1)} async-done(((f32[8,1,256]{2,1,0:T(1,128)}), f32[8,1,256]{2,1,0:T(1,128)S(1)}, u32[]{:S(2)}, u32[]{:S(2)}) %all-to-all-start.6) | async-done | bytes 8224 | tf_op jit(solution)/shard_map/all_to_all | solution.py:12
  144.8 9.8 %all_to_all.96 = f32[16,1,512]{2,1,0:T(1,128)S(1)} all-to-all(f32[16,1,512]{2,1,0:T(1,128)S(1)} %all_to_all.81), channel_id=1, replica_groups=mesh['src'=8,'tgt'=16] {'tgt'}, dimensions={0} | all-to-all | bytes 65536 | tf_op jit(solution)/shard_map/all_to_all | solution.py:12
  154.7 2.2 %convolution_convert_fusion = bf16[512,2048]{1,0:T(8,128)(2,1)} fusion(bf16[256,2048]{1,0:T(8,128)(2,1)S(1)} %copy-done.1, f32[512,256]{0,1:T(8,128)S(1)} %get-tuple-element.11, f32[512]{0:T(512)S(1)} %log_add_fusion, f32[256]{0:T(256)S(1)} %add_multiply_fusion.3), kind=kOutput, calls=%fused_computation.4 | convolution fusion | flops 538443776 | bytes 3673088 | tf_op jit(solution)/shard_map/dot_general | solution.py:64
  156.9 5.8 %all-to-all-start.8 = ((bf16[16,32,2048]{2,1,0:T(8,128)(2,1)}), bf16[16,32,2048]{2,1,0:T(8,128)(2,1)}, u32[]{:S(2)}, u32[]{:S(2)}) async-start(bf16[16,32,2048]{2,1,0:T(8,128)(2,1)} %bitcast.54), calls=%async_computation.8 | async-start | bytes 4194304 | tf_op jit(solution)/shard_map/all_to_all | solution.py:65
  162.7 33.2 %all-to-all-done.8 = bf16[16,32,2048]{2,1,0:T(8,128)(2,1)} async-done(((bf16[16,32,2048]{2,1,0:T(8,128)(2,1)}), bf16[16,32,2048]{2,1,0:T(8,128)(2,1)}, u32[]{:S(2)}, u32[]{:S(2)}) %all-to-all-start.8) | async-done | bytes 2097184 | tf_op jit(solution)/shard_map/all_to_all | solution.py:65
  195.9 2.0 convert_reduce_fusion
  197.9 0.7 fusion.23
  199.1 1.3 multiply_reduce_fusion
  200.6 8.5 %multiply_convert_fusion = bf16[1024,6144]{1,0:T(8,128)(2,1)} fusion(f32[1024]{0:T(1024)S(1)} %rsqrt.11, bf16[192,6144]{1,0:T(8,128)(2,1)} %all-gather.5.cloned.1.call-done, bf16[1024,32]{1,0:T(8,128)(2,1)S(1)} %bitcast.55, bf16[1024,64]{1,0:T(8,128)(2,1)S(1)} %reshape.169), kind=kOutput, calls=%fused_computation | convolution fusion | flops 2430074880 | bytes 15142912 | tf_op jit(solution)/shard_map/dot_general | solution.py:81
  (80 shorter events, 4.3 us)
Async XLA Ops:
  8.0 107.2 %copy-start = (bf16[2048,384]{1,0:T(8,128)(2,1)S(1)}, bf16[2048,384]{1,0:T(8,128)(2,1)}, u32[]{:S(2)}) copy-start(bf16[2048,384]{1,0:T(8,128)(2,1)} %param.13) | copy-start | bytes 4718596
  8.0 61.2 %all-gather.3.cloned.1.call-start = ((), (), s32[]{:S(2)}) async-start(), calls=%async_computation.9 | async-start | bytes 1179648 | tf_op jit(solution)/shard_map/all_gather | solution.py:46
  11.2 59.6 %all-to-all-start = ((bf16[16,32,2048]{2,1,0:T(8,128)(2,1)}), bf16[16,32,2048]{2,1,0:T(8,128)(2,1)}, u32[]{:S(2)}, u32[]{:S(2)}) async-start(bf16[16,32,2048]{2,1,0:T(8,128)(2,1)} %stack.2), calls=%async_computation | async-start | bytes 4194304 | tf_op jit(solution)/shard_map/all_to_all | solution.py:44
  69.3 3.8 %copy-start.1 = (bf16[256,2048]{1,0:T(8,128)(2,1)S(1)}, bf16[256,2048]{1,0:T(8,128)(2,1)}, u32[]{:S(2)}) copy-start(bf16[256,2048]{1,0:T(8,128)(2,1)} %all-gather.3.cloned.1.call-done) | copy-start | bytes 3145732
  75.4 30.6 %copy-start.2 = (bf16[32,2048]{1,0:T(8,128)(2,1)S(1)}, bf16[32,2048]{1,0:T(8,128)(2,1)}, u32[]{:S(2)}) copy-start(bf16[32,2048]{1,0:T(8,128)(2,1)} %param.11) | copy-start | bytes 393220
  75.4 30.6 %copy-start.5 = (f32[2048]{0:T(1024)S(1)}, f32[2048]{0:T(1024)}, u32[]{:S(2)}) copy-start(f32[2048]{0:T(1024)} %param.12) | copy-start | bytes 24580
  99.2 11.6 %all-to-all-start.3 = ((f32[16,1,512]{2,1,0:T(1,128)}), f32[16,1,512]{2,1,0:T(1,128)S(1)}, u32[]{:S(2)}, u32[]{:S(2)}) async-start(f32[16,1,512]{2,1,0:T(1,128)} %all_to_all.69), calls=%async_computation.3 | async-start | bytes 65536 | tf_op jit(solution)/shard_map/all_to_all | solution.py:12
  111.9 9.8 %all-to-all-start.4 = ((f32[8,1,256]{2,1,0:T(1,128)}), f32[8,1,256]{2,1,0:T(1,128)S(1)}, u32[]{:S(2)}, u32[]{:S(2)}) async-start(f32[8,1,256]{2,1,0:T(1,128)} %all_to_all.72), calls=%async_computation.4 | async-start | bytes 16384 | tf_op jit(solution)/shard_map/all_to_all | solution.py:12
  122.7 10.7 %all-to-all-start.5 = ((f32[16,1,512]{2,1,0:T(1,128)}), f32[16,1,512]{2,1,0:T(1,128)S(1)}, u32[]{:S(2)}, u32[]{:S(2)}) async-start(f32[16,1,512]{2,1,0:T(1,128)} %all_to_all.75), calls=%async_computation.5 | async-start | bytes 65536 | tf_op jit(solution)/shard_map/all_to_all | solution.py:12
  134.5 9.8 %all-to-all-start.6 = ((f32[8,1,256]{2,1,0:T(1,128)}), f32[8,1,256]{2,1,0:T(1,128)S(1)}, u32[]{:S(2)}, u32[]{:S(2)}) async-start(f32[8,1,256]{2,1,0:T(1,128)} %all_to_all.78), calls=%async_computation.6 | async-start | bytes 16384 | tf_op jit(solution)/shard_map/all_to_all | solution.py:12
  137.9 62.7 %all-gather.5.cloned.1.call-start = ((), (), s32[]{:S(2)}) async-start(), calls=%async_computation.10 | async-start | bytes 2506752 | tf_op jit(solution)/shard_map/all_gather | solution.py:40
  156.9 5.8 %copy-start.6 = (s32[32]{0:T(128)S(1)}, s32[32]{0:T(128)}, u32[]{:S(2)}) copy-start(s32[32]{0:T(128)} %param.9) | copy-start | bytes 388
  156.9 39.0 %all-to-all-start.8 = ((bf16[16,32,2048]{2,1,0:T(8,128)(2,1)}), bf16[16,32,2048]{2,1,0:T(8,128)(2,1)}, u32[]{:S(2)}, u32[]{:S(2)}) async-start(bf16[16,32,2048]{2,1,0:T(8,128)(2,1)} %bitcast.54), calls=%async_computation.8 | async-start | bytes 4194304 | tf_op jit(solution)/shard_map/all_to_all | solution.py:65
  162.7 35.3 %copy-start.3 = (bf16[32,2048]{1,0:T(8,128)(2,1)S(1)}, bf16[32,2048]{1,0:T(8,128)(2,1)}, u32[]{:S(2)}) copy-start(bf16[32,2048]{1,0:T(8,128)(2,1)} %param.7) | copy-start | bytes 393220
  162.7 36.5 %copy-start.4 = (bf16[64,2048]{1,0:T(8,128)(2,1)S(1)}, bf16[64,2048]{1,0:T(8,128)(2,1)}, u32[]{:S(2)}) copy-start(bf16[64,2048]{1,0:T(8,128)(2,1)} %param.10) | copy-start | bytes 786436
Sparse Core Ops, SparseCore 0:
  11.2 58.0 all-gather.2
Sparse Core Ops, SparseCore 1:
  140.0 46.7 all-gather.4
